TPU v7x, 32 devices: a whole 2x2x4 slice. The times are simulated.
32 devices in a mesh: coarse: 4 (over y, x), fine: 8 (over z, core).
Axes of the slice: x: 2, y: 2, z: 4, core: 2. Of those that a mesh axis runs over, the one named last changes fastest.
Arguments:
- embeddings: bfloat16 [16384, 512], P(('coarse', 'fine')), may hold values from -64 to 64
- labels: int32 [16384, 1], P(('coarse', 'fine')), may hold values from 0 to 7; in each aligned block of 512 rows (0 to 511, 512 to 1023, ...) at most 128 rows name the same one
Outputs:
- max_similarity: float32 [16384], P(('coarse', 'fine'))
Inputs may be any that keep to these rules, and one draw needn't show every extreme that they name: `labels`: among the rows of one device no label appears more than 128 times; on some device one label appears exactly 128 times.
All inputs are finite; a program needn't handle non-finite values. Where the computation divides by a largest or mean magnitude, that divisor is 1e-20 or more.
Results may differ from a plain program's by a relative error of at most 0.00035.
The roundings to bfloat16 on the way count: a program that leaves them out, or rounds other values in their place, can miss the bound.
Values may be sent and summed in bfloat16 or wider, within the bound.
A program may use at most 64 MiB of HBM per device.

v0:
```python
import functools

import jax
import jax.numpy as jnp
from jax import lax
from jax.experimental import pallas as pl
from jax.experimental.pallas import tpu as pltpu
from jax.sharding import PartitionSpec as P

EPS = 1e-06
RIDGE = 0.001
LANES = 128
LOW = -3.0e38
MESH = pl.DeviceIdType.MESH


def dot(left, right):
    return jnp.dot(left, right, preferred_element_type=jnp.float32)


def split_two(value):
    high = value.astype(jnp.bfloat16)
    return high, (value - high.astype(jnp.float32)).astype(jnp.bfloat16)


def dot_split(left, right):
    left_high, left_low = left
    right_high, right_low = right
    return dot(left_high, right_high) + (dot(left_high, right_low) + dot(left_low, right_high))


def remote(src, dst, send_sem, recv_sem, device):
    return pltpu.make_async_remote_copy(
        src_ref=src, dst_ref=dst, send_sem=send_sem, recv_sem=recv_sem,
        device_id=device, device_id_type=MESH,
    )


def rows_at(ref, start, size):
    return ref.at[pl.ds(pl.multiple_of(start, 8), size)]


def kernel(
    C, F, slot, stack_rows, row_total,
    emb_hbm, labels_hbm, out,
    emb, labels, acc, half_in, half, coarse_in, part, z_in, total,
    outgoing, received, counts_out, counts_in, full, whiten, unit, best, returned,
    emb_sem, labels_sem,    core_s, core_r, coarse_s, coarse_r, z_s, z_r, gz_s, gz_r, gc_s, gc_r, gk_s, gk_r,
    a_s, a_r, n_s, n_r, b_s, b_r,
):
    emb_copy = pltpu.make_async_copy(emb_hbm, emb, emb_sem)
    labels_copy = pltpu.make_async_copy(labels_hbm, labels, labels_sem)
    emb_copy.start()
    labels_copy.start()
    rows, width = emb.shape
    blocks = width // LANES
    pairs = [(i, j) for i in range(blocks) for j in range(i, blocks)]
    Z = F // 2
    slots = F * slot
    c = lax.axis_index("coarse")
    f = lax.axis_index("fine")
    core = lax.rem(f, 2)
    z = lax.div(f, 2)
    sibling = (c, f + 1 - 2 * core)

    def fine_peer(k):
        return lax.rem(f + k, F)

    def coarse_peer(k):
        return lax.rem(c + k, C)

    def z_peer(k):
        return lax.rem(z + k, Z)

    def z_other(k, flip):
        return 2 * z_peer(k) + (1 - core if flip else core)

    steps = sorted(range(1, Z), key=lambda k: -min(k, Z - k))
    first = [z_other(k, False) for k in steps] + [z_other(0, True)]
    second_lot = [z_other(k, True) for k in steps]
    peers = first + second_lot

    barrier = pltpu.get_barrier_semaphore()
    for k in range(1, F):
        pl.semaphore_signal(barrier, inc=1, device_id=(c, fine_peer(k)), device_id_type=MESH)
    for k in range(1, C):
        pl.semaphore_signal(barrier, inc=1, device_id=(coarse_peer(k), f), device_id_type=MESH)

    emb_copy.wait()
    used = len(pairs) * LANES
    if stack_rows > used:
        acc[used:, :] = jnp.zeros((stack_rows - used, LANES), jnp.float32)
    place = 0
    for i in range(blocks):
        strip = lax.dot_general(
            emb[:, i * LANES:(i + 1) * LANES], emb[:, i * LANES:],
            (((0,), (0,)), ((), ())), preferred_element_type=jnp.float32,
        )
        for j in range(blocks - i):
            acc[place * LANES:(place + 1) * LANES, :] = strip[:, j * LANES:(j + 1) * LANES]
            place += 1
    pl.semaphore_wait(barrier, F + C - 2)

    half_rows = stack_rows // 2
    part_rows = half_rows // C
    piece_rows = part_rows // Z

    core_copy = remote(
        rows_at(acc, (1 - core) * half_rows, half_rows), half_in, core_s, core_r, sibling
    )
    core_copy.start()

    labels_copy.wait()
    label_row = labels[...]
    onehot = lax.broadcasted_iota(jnp.int32, (F, rows), 0) == label_row
    before = (
        lax.broadcasted_iota(jnp.int32, (rows, rows), 0)
        < lax.broadcasted_iota(jnp.int32, (rows, rows), 1)
    )
    flags = jnp.where(onehot, 1.0, 0.0)
    rank_all = dot(flags.astype(jnp.bfloat16), jnp.where(before, 1.0, 0.0).astype(jnp.bfloat16))
    rank = jnp.sum(jnp.where(onehot, rank_all, 0.0), axis=0, keepdims=True).astype(jnp.int32)
    amounts = jnp.sum(flags, axis=1, keepdims=True)
    for label in range(F):
        counts_out[label] = jnp.broadcast_to(amounts[label:label + 1, :], (8, LANES))
    slot_of = label_row * slot + rank
    step = min(256, slots)
    for start in range(0, slots, step):
        pick = lax.broadcasted_iota(jnp.int32, (step, rows), 0) + start == slot_of
        outgoing[start:start + step, :] = dot(
            jnp.where(pick, 1.0, 0.0).astype(jnp.bfloat16), emb[...]
        ).astype(jnp.bfloat16)

    def slot_rows(ref, which):
        return ref.at[pl.ds(pl.multiple_of(which * slot, 16), slot)]

    def row_copy(to, source):
        return remote(
            slot_rows(outgoing, to), slot_rows(received, source), a_s.at[to], a_r.at[source], (c, to)
        )

    def count_copy(to, source):
        return remote(counts_out.at[to], counts_in.at[source], n_s.at[to], n_r.at[source], (c, to))

    for k in range(1, F):
        count_copy(fine_peer(k), f).start()

    core_copy.wait_recv()
    half[...] = rows_at(acc, core * half_rows, half_rows)[...] + half_in[...]

    def coarse_copy(to, source):
        return remote(
            rows_at(half, to * part_rows, part_rows), coarse_in.at[source],
            coarse_s.at[to], coarse_r.at[source], (to, f),
        )

    for k in range(1, C):
        coarse_copy(coarse_peer(k), c).start()
    for peer in first:
        row_copy(peer, f).start()
    value = rows_at(half, c * part_rows, part_rows)[...]
    for k in range(1, C):
        coarse_copy(coarse_peer(k), coarse_peer(k)).wait_recv()
        value = value + coarse_in[coarse_peer(k)]
    part[...] = value

    def z_copy(to, source):
        return remote(
            rows_at(part, to * piece_rows, piece_rows), z_in.at[source],
            z_s.at[to], z_r.at[source], (c, 2 * to + core),
        )

    for k in range(1, Z):
        z_copy(z_peer(k), z).start()
    value = rows_at(part, z * piece_rows, piece_rows)[...]
    for k in range(1, Z):
        z_copy(z_peer(k), z_peer(k)).wait_recv()
        value = value + z_in[z_peer(k)]

    def piece_start(coarse_id, z_id):
        return core * half_rows + coarse_id * part_rows + z_id * piece_rows

    rows_at(total, piece_start(c, z), piece_rows)[...] = value

    def z_gather(to, source):
        piece = rows_at(total, piece_start(c, source), piece_rows)
        return remote(piece, piece, gz_s.at[to], gz_r.at[source], (c, 2 * to + core))

    def coarse_gather(to, source):
        piece = rows_at(total, piece_start(source, 0), part_rows)
        return remote(piece, piece, gc_s.at[to], gc_r.at[source], (to, f))

    def core_gather(source):
        piece = rows_at(total, source * half_rows, half_rows)
        return remote(piece, piece, gk_s, gk_r, sibling)

    for k in range(1, Z):
        z_gather(z_peer(k), z).start()
    for peer in second_lot:
        row_copy(peer, f).start()
    for k in range(1, Z):
        z_gather(z_peer(k), z_peer(k)).wait_recv()
    for k in range(1, C):
        coarse_gather(coarse_peer(k), c).start()
    for k in range(1, C):
        coarse_gather(coarse_peer(k), coarse_peer(k)).wait_recv()
    core_gather(core).start()

    slot_rows(received, f)[...] = slot_rows(outgoing, f)[...]
    counts_in[f] = counts_out[f]
    for k in range(1, F):
        count_copy(fine_peer(k), fine_peer(k)).wait_recv()

    core_gather(1 - core).wait_recv()
    for place, (i, j) in enumerate(pairs):
        block = total[place * LANES:(place + 1) * LANES, :] / row_total
        if i == j:
            diagonal = (
                lax.broadcasted_iota(jnp.int32, (LANES, LANES), 0)
                == lax.broadcasted_iota(jnp.int32, (LANES, LANES), 1)
            )
            block = block + jnp.where(diagonal, RIDGE, 0.0)
        else:
            full[j * LANES:(j + 1) * LANES, i * LANES:(i + 1) * LANES] = block.T
        full[i * LANES:(i + 1) * LANES, j * LANES:(j + 1) * LANES] = block
    second = full[...]
    norm_scale = jnp.max(jnp.sum(jnp.abs(second), axis=0, keepdims=True), axis=1, keepdims=True)
    root = second / norm_scale
    identity = jnp.where(
        lax.broadcasted_iota(jnp.int32, (width, width), 0)
        == lax.broadcasted_iota(jnp.int32, (width, width), 1),
        1.0, 0.0,
    )
    root_parts = split_two(root)
    square = dot_split(root_parts, root_parts)
    outer = 1.6875 * identity - 0.5625 * root + 0.0625 * square
    inverse = 2.25 * identity - 2.4375 * root + dot_split(split_two(square), split_two(outer))
    whiten[...] = (inverse / jnp.sqrt(norm_scale)).astype(jnp.bfloat16)

    group = LANES // slot
    if group == 1:
        order = [f] + peers
    else:
        order = [lax.rem(lax.div(f, group) + n, F // group) for n in range(F // group)]
        for peer in peers:
            row_copy(peer, peer).wait_recv()
    rank_here = lax.broadcasted_iota(jnp.int32, (slot, LANES), 0).astype(jnp.float32)
    diagonal = (
        lax.broadcasted_iota(jnp.int32, (LANES, LANES), 0)
        == lax.broadcasted_iota(jnp.int32, (LANES, LANES), 1)
    )

    def highest(tile):
        return jnp.max(tile.reshape(LANES // 8, 8, LANES), axis=0)

    tops, biases = [], []
    for n, block in enumerate(order):
        if group == 1 and n > 0:
            row_copy(block, block).wait_recv()
        white = dot(rows_at(received, block * LANES, LANES)[...], whiten[...])
        meansq = jnp.mean(white * white, axis=-1, keepdims=True)
        here = (white * lax.rsqrt(width * (meansq + EPS))).astype(jnp.bfloat16)
        unit[n * LANES:(n + 1) * LANES, :] = here
        bias = [
            jnp.where(rank_here < counts_in[block * group + m][0:1, :], 0.0, LOW) for m in range(group)
        ]
        bias = bias[0] if group == 1 else jnp.concatenate(bias, axis=0)
        so_far = unit[0:(n + 1) * LANES, :]
        down = lax.dot_general(here, so_far, (((1,), (1,)), ((), ())), preferred_element_type=jnp.float32)
        for t in range(n):
            tops[t] = jnp.maximum(tops[t], highest(down[:, t * LANES:(t + 1) * LANES] + bias))
        top = highest(jnp.where(diagonal, LOW, down[:, n * LANES:] + bias))
        if n > 0:
            across = lax.dot_general(
                unit[0:n * LANES, :], here, (((1,), (1,)), ((), ())), preferred_element_type=jnp.float32
            )
            for t in range(n):
                top = jnp.maximum(top, highest(across[t * LANES:(t + 1) * LANES, :] + biases[t]))
        tops.append(jnp.maximum(top, -1.0))
        biases.append(bias)
    for n, block in enumerate(order):
        best[block] = jnp.broadcast_to(jnp.max(tops[n], axis=0, keepdims=True), (8, LANES))

    def best_copy(to, source):
        return remote(
            best.at[lax.div(to, group)], returned.at[source], b_s.at[to], b_r.at[source], (c, to)
        )

    for peer in peers:
        best_copy(peer, f).start()
    returned[f] = best[lax.div(f, group)]
    pick = lax.broadcasted_iota(jnp.int32, (LANES, rows), 0) == rank + lax.rem(f * slot, LANES)
    pick = jnp.where(pick, 1.0, 0.0).astype(jnp.bfloat16)
    mine = lax.broadcasted_iota(jnp.int32, (F * 8, rows), 0) == label_row * 8
    for k in range(1, F):
        best_copy(fine_peer(k), fine_peer(k)).wait_recv()
    values = returned[...].reshape(F * 8, LANES)
    high, rest = values.astype(jnp.bfloat16), None
    rest = values - high.astype(jnp.float32)
    middle, low = split_two(rest)
    found = dot(high, pick) + (dot(middle, pick) + dot(low, pick))
    out[...] = jnp.sum(jnp.where(mine, found, 0.0), axis=0, keepdims=True)

    core_copy.wait_send()
    core_gather(core).wait_send()
    for k in range(1, C):
        coarse_copy(coarse_peer(k), c).wait_send()
        coarse_gather(coarse_peer(k), c).wait_send()
    for k in range(1, Z):
        z_copy(z_peer(k), z).wait_send()
        z_gather(z_peer(k), z).wait_send()
    for k in range(1, F):
        row_copy(fine_peer(k), f).wait_send()
        count_copy(fine_peer(k), f).wait_send()
        best_copy(fine_peer(k), f).wait_send()


def per_device(embeddings, labels):
    rows, width = embeddings.shape
    F = lax.axis_size("fine")
    C = lax.axis_size("coarse")
    Z = F // 2
    slot = 2 * rows // F
    slots = F * slot
    blocks = width // LANES
    unit_rows = 8 * C * F
    stack_rows = -(-(blocks * (blocks + 1) // 2 * LANES) // unit_rows) * unit_rows
    half_rows = stack_rows // 2
    part_rows = half_rows // C
    piece_rows = part_rows // Z
    f32, bf16 = jnp.float32, jnp.bfloat16
    dma = pltpu.SemaphoreType.DMA
    best = pl.pallas_call(
        functools.partial(kernel, C, F, slot, stack_rows, rows * F * C),
        out_shape=jax.ShapeDtypeStruct((1, rows), f32),
        in_specs=[pl.BlockSpec(memory_space=pl.ANY)] * 2,
        out_specs=pl.BlockSpec(memory_space=pltpu.VMEM),
        scratch_shapes=[
            pltpu.VMEM((rows, width), bf16),
            pltpu.VMEM((1, rows), jnp.int32),
            pltpu.VMEM((stack_rows, LANES), f32),
            pltpu.VMEM((half_rows, LANES), f32),
            pltpu.VMEM((half_rows, LANES), f32),
            pltpu.VMEM((C, part_rows, LANES), f32),
            pltpu.VMEM((part_rows, LANES), f32),
            pltpu.VMEM((Z, piece_rows, LANES), f32),
            pltpu.VMEM((stack_rows, LANES), f32),
            pltpu.VMEM((slots, width), bf16),
            pltpu.VMEM((slots, width), bf16),
            pltpu.VMEM((F, 8, LANES), f32),
            pltpu.VMEM((F, 8, LANES), f32),
            pltpu.VMEM((width, width), f32),
            pltpu.VMEM((width, width), bf16),
            pltpu.VMEM((slots, width), bf16),
            pltpu.VMEM((slots // LANES, 8, LANES), f32),
            pltpu.VMEM((F, 8, LANES), f32),
            dma, dma,
            dma, dma, dma((C,)), dma((C,)), dma((Z,)), dma((Z,)),
            dma((Z,)), dma((Z,)), dma((C,)), dma((C,)), dma, dma,
            dma((F,)), dma((F,)), dma((F,)), dma((F,)), dma((F,)), dma((F,)),
        ],
        compiler_params=pltpu.CompilerParams(
            collective_id=0, has_side_effects=True, vmem_limit_bytes=60 * 1024 * 1024
        ),
    )(embeddings, labels.reshape(1, rows))
    return best.reshape(rows)


def solution(mesh):
    in_specs = (P(("coarse", "fine"), None), P(("coarse", "fine"), None))
    out_specs = P(("coarse", "fine"))
    return jax.shard_map(
        per_device, mesh=mesh, in_specs=in_specs, out_specs=out_specs, check_vma=False
    )
```

profile of v0, /device:TPU:0, one launch (start us, length us, event | category | flops | bytes accessed | tf_op | source)
XLA Modules:
  0.0 50.0 jit_solution(799803338260048576)
XLA Ops:
  0.0 48.7 %shard_map.28 = f32[1,512]{1,0:T(1,128)} custom-call(bf16[512,512]{1,0:T(8,128)(2,1)} %emb_hbm.1, s32[1,512]{1,0:T(1,128)} %bitcast.3), custom_call_target="tpu_custom_call" | custom-call | tf_op jit(solution)/shard_map/pallas_call | solution.py:333
  48.7 1.3 %copy.4 = f32[512]{0:T(512)} copy(f32[512]{0:T(512)} %bitcast.2) | data formatting | bytes 4096
where the time goes:
time: 50.1 us; the launch traced here: 50 us
  Pallas kernels  48.7 us (97%)
  local copies, waits for them, and re-layouts  1.26 us (3%)
    pallas_call x1, Pallas kernels, per_device(): pl.pallas_call(functools.partial(kernel, C, F, slot, stack_rows, rows * F...  48.7 us
    unnamed x1, local copies, waits for them, and re-layouts  1.26 us

commit v1 on v0

--- a/solution.py
+++ b/solution.py
@@ -21,12 +21,6 @@
 def split_two(value):
     high = value.astype(jnp.bfloat16)
     return high, (value - high.astype(jnp.float32)).astype(jnp.bfloat16)
-
-
-def dot_split(left, right):
-    left_high, left_low = left
-    right_high, right_low = right
-    return dot(left_high, right_high) + (dot(left_high, right_low) + dot(left_low, right_high))
 
 
 def remote(src, dst, send_sem, recv_sem, device):
@@ -75,10 +69,11 @@
     def z_other(k, flip):
         return 2 * z_peer(k) + (1 - core if flip else core)
 
-    steps = sorted(range(1, Z), key=lambda k: -min(k, Z - k))
-    first = [z_other(k, False) for k in steps] + [z_other(0, True)]
-    second_lot = [z_other(k, True) for k in steps]
-    peers = first + second_lot
+    steps = sorted(range(1, Z), key=lambda k: min(k, Z - k))
+    far = [z_other(k, flip) for k in steps for flip in (False, True)]
+    early, middle = len(far) // 3, len(far) // 3 + len(far) // 6
+    lots = [far[:early] + [z_other(0, True)], far[early:middle], far[middle + 1:] + [far[middle]]]
+    peers = lots[0] + lots[1] + lots[2]
 
     barrier = pltpu.get_barrier_semaphore()
     for k in range(1, F):
@@ -124,13 +119,6 @@
     for label in range(F):
         counts_out[label] = jnp.broadcast_to(amounts[label:label + 1, :], (8, LANES))
     slot_of = label_row * slot + rank
-    step = min(256, slots)
-    for start in range(0, slots, step):
-        pick = lax.broadcasted_iota(jnp.int32, (step, rows), 0) + start == slot_of
-        outgoing[start:start + step, :] = dot(
-            jnp.where(pick, 1.0, 0.0).astype(jnp.bfloat16), emb[...]
-        ).astype(jnp.bfloat16)
-
     def slot_rows(ref, which):
         return ref.at[pl.ds(pl.multiple_of(which * slot, 16), slot)]
 
@@ -142,8 +130,16 @@
     def count_copy(to, source):
         return remote(counts_out.at[to], counts_in.at[source], n_s.at[to], n_r.at[source], (c, to))
 
-    for k in range(1, F):
-        count_copy(fine_peer(k), f).start()
+    def compact(devices):
+        places = lax.broadcasted_iota(jnp.int32, (slot, rows), 0)
+        picks = [
+            jnp.where(places + to * slot == slot_of, 1.0, 0.0).astype(jnp.bfloat16) for to in devices
+        ]
+        picked = dot(jnp.concatenate(picks, axis=0), emb[...]).astype(jnp.bfloat16)
+        for n, to in enumerate(devices):
+            slot_rows(outgoing, to)[...] = picked[n * slot:(n + 1) * slot, :]
+
+    compact(lots[0])
 
     core_copy.wait_recv()
     half[...] = rows_at(acc, core * half_rows, half_rows)[...] + half_in[...]
@@ -156,8 +152,13 @@
 
     for k in range(1, C):
         coarse_copy(coarse_peer(k), c).start()
-    for peer in first:
+    for peer in lots[0]:
         row_copy(peer, f).start()
+    for peer in peers:
+        count_copy(peer, f).start()
+    compact(lots[1] + lots[2] + [f])
+    slot_rows(received, f)[...] = slot_rows(outgoing, f)[...]
+    counts_in[f] = counts_out[f]
     value = rows_at(half, c * part_rows, part_rows)[...]
     for k in range(1, C):
         coarse_copy(coarse_peer(k), coarse_peer(k)).wait_recv()
@@ -172,6 +173,8 @@
 
     for k in range(1, Z):
         z_copy(z_peer(k), z).start()
+    for peer in lots[1]:
+        row_copy(peer, f).start()
     value = rows_at(part, z * piece_rows, piece_rows)[...]
     for k in range(1, Z):
         z_copy(z_peer(k), z_peer(k)).wait_recv()
@@ -196,7 +199,7 @@
 
     for k in range(1, Z):
         z_gather(z_peer(k), z).start()
-    for peer in second_lot:
+    for peer in lots[2]:
         row_copy(peer, f).start()
     for k in range(1, Z):
         z_gather(z_peer(k), z_peer(k)).wait_recv()
@@ -206,14 +209,12 @@
         coarse_gather(coarse_peer(k), coarse_peer(k)).wait_recv()
     core_gather(core).start()
 
-    slot_rows(received, f)[...] = slot_rows(outgoing, f)[...]
-    counts_in[f] = counts_out[f]
     for k in range(1, F):
         count_copy(fine_peer(k), fine_peer(k)).wait_recv()
 
     core_gather(1 - core).wait_recv()
     for place, (i, j) in enumerate(pairs):
-        block = total[place * LANES:(place + 1) * LANES, :] / row_total
+        block = total[place * LANES:(place + 1) * LANES, :] * (1.0 / row_total)
         if i == j:
             diagonal = (
                 lax.broadcasted_iota(jnp.int32, (LANES, LANES), 0)
@@ -225,17 +226,17 @@
         full[i * LANES:(i + 1) * LANES, j * LANES:(j + 1) * LANES] = block
     second = full[...]
     norm_scale = jnp.max(jnp.sum(jnp.abs(second), axis=0, keepdims=True), axis=1, keepdims=True)
-    root = second / norm_scale
+    root = second * (1.0 / norm_scale)
     identity = jnp.where(
         lax.broadcasted_iota(jnp.int32, (width, width), 0)
         == lax.broadcasted_iota(jnp.int32, (width, width), 1),
-        1.0, 0.0,
-    )
-    root_parts = split_two(root)
-    square = dot_split(root_parts, root_parts)
-    outer = 1.6875 * identity - 0.5625 * root + 0.0625 * square
-    inverse = 2.25 * identity - 2.4375 * root + dot_split(split_two(square), split_two(outer))
-    whiten[...] = (inverse / jnp.sqrt(norm_scale)).astype(jnp.bfloat16)
+        2.25, 0.0,
+    )
+    root_b = root.astype(jnp.bfloat16)
+    square = dot(root_b, root_b)
+    outer = (0.0625 * square - 0.5625 * root).astype(jnp.bfloat16)
+    inverse = identity - 2.4375 * root + 1.6875 * square + dot(square.astype(jnp.bfloat16), outer)
+    whiten[...] = (inverse * (1.0 / jnp.sqrt(norm_scale))).astype(jnp.bfloat16)
 
     group = LANES // slot
     if group == 1:
@@ -360,7 +361,7 @@
             dma((F,)), dma((F,)), dma((F,)), dma((F,)), dma((F,)), dma((F,)),
         ],
         compiler_params=pltpu.CompilerParams(
-            collective_id=0, has_side_effects=True, vmem_limit_bytes=60 * 1024 * 1024
+            collective_id=0, has_side_effects=True, vmem_limit_bytes=(64 * 1024 - 256) * 1024
         ),
     )(embeddings, labels.reshape(1, rows))
     return best.reshape(rows)

time: 50.1 us -> 50.3 us (level)
  no operation moved by 1% of the time
where the time goes in v1:
time: 50.3 us; the launch traced here: 50.1 us
  Pallas kernels  48.9 us (97%)
  local copies, waits for them, and re-layouts  1.26 us (3%)
    pallas_call x1, Pallas kernels, per_device(): pl.pallas_call(functools.partial(kernel, C, F, slot, stack_rows, rows * F...  48.9 us
    unnamed x1, local copies, waits for them, and re-layouts  1.26 us

profile of v1, /device:TPU:0, one launch (start us, length us, event | category | flops | bytes accessed | tf_op | source)
XLA Modules:
  0.0 50.1 jit_solution(14828485237135488546)
XLA Ops:
  0.0 48.9 %shard_map.28 = f32[1,512]{1,0:T(1,128)} custom-call(bf16[512,512]{1,0:T(8,128)(2,1)} %emb_hbm.1, s32[1,512]{1,0:T(1,128)} %bitcast.3), custom_call_target="tpu_custom_call" | custom-call | tf_op jit(solution)/shard_map/pallas_call | solution.py:334
  48.9 1.3 %copy.4 = f32[512]{0:T(512)} copy(f32[512]{0:T(512)} %bitcast.2) | data formatting | bytes 4096

commit v2 on v1

--- a/solution.py
+++ b/solution.py
@@ -240,11 +240,12 @@
 
     group = LANES // slot
     if group == 1:
-        order = [f] + peers
+        batches = [[f] + lots[0] + lots[1], lots[2]]
     else:
-        order = [lax.rem(lax.div(f, group) + n, F // group) for n in range(F // group)]
+        batches = [[lax.rem(lax.div(f, group) + n, F // group) for n in range(F // group)]]
         for peer in peers:
             row_copy(peer, peer).wait_recv()
+    order = sum(batches, [])
     rank_here = lax.broadcasted_iota(jnp.int32, (slot, LANES), 0).astype(jnp.float32)
     diagonal = (
         lax.broadcasted_iota(jnp.int32, (LANES, LANES), 0)
@@ -254,31 +255,42 @@
     def highest(tile):
         return jnp.max(tile.reshape(LANES // 8, 8, LANES), axis=0)
 
-    tops, biases = [], []
-    for n, block in enumerate(order):
-        if group == 1 and n > 0:
-            row_copy(block, block).wait_recv()
-        white = dot(rows_at(received, block * LANES, LANES)[...], whiten[...])
+    tops, biases, done = [], [], 0
+    for batch in batches:
+        if group == 1:
+            for block in batch:
+                if block is not f:
+                    row_copy(block, block).wait_recv()
+        arrived = [rows_at(received, block * LANES, LANES)[...] for block in batch]
+        white = dot(jnp.concatenate(arrived, axis=0), whiten[...])
         meansq = jnp.mean(white * white, axis=-1, keepdims=True)
         here = (white * lax.rsqrt(width * (meansq + EPS))).astype(jnp.bfloat16)
-        unit[n * LANES:(n + 1) * LANES, :] = here
-        bias = [
-            jnp.where(rank_here < counts_in[block * group + m][0:1, :], 0.0, LOW) for m in range(group)
-        ]
-        bias = bias[0] if group == 1 else jnp.concatenate(bias, axis=0)
-        so_far = unit[0:(n + 1) * LANES, :]
-        down = lax.dot_general(here, so_far, (((1,), (1,)), ((), ())), preferred_element_type=jnp.float32)
-        for t in range(n):
-            tops[t] = jnp.maximum(tops[t], highest(down[:, t * LANES:(t + 1) * LANES] + bias))
-        top = highest(jnp.where(diagonal, LOW, down[:, n * LANES:] + bias))
-        if n > 0:
+        end = done + len(batch)
+        unit[done * LANES:end * LANES, :] = here
+        for block in batch:
+            bias = [
+                jnp.where(rank_here < counts_in[block * group + m][0:1, :], 0.0, LOW) for m in range(group)
+            ]
+            biases.append(bias[0] if group == 1 else jnp.concatenate(bias, axis=0))
+            tops.append(jnp.full((8, LANES), -1.0, jnp.float32))
+        down = lax.dot_general(
+            here, unit[0:end * LANES, :], (((1,), (1,)), ((), ())), preferred_element_type=jnp.float32
+        )
+        for q in range(done, end):
+            for t in range(end):
+                tile = down[(q - done) * LANES:(q - done + 1) * LANES, t * LANES:(t + 1) * LANES] + biases[q]
+                if t == q:
+                    tile = jnp.where(diagonal, LOW, tile)
+                tops[t] = jnp.maximum(tops[t], highest(tile))
+        if done > 0:
             across = lax.dot_general(
-                unit[0:n * LANES, :], here, (((1,), (1,)), ((), ())), preferred_element_type=jnp.float32
+                unit[0:done * LANES, :], here, (((1,), (1,)), ((), ())), preferred_element_type=jnp.float32
             )
-            for t in range(n):
-                top = jnp.maximum(top, highest(across[t * LANES:(t + 1) * LANES, :] + biases[t]))
-        tops.append(jnp.maximum(top, -1.0))
-        biases.append(bias)
+            for q in range(done):
+                for t in range(done, end):
+                    tile = across[q * LANES:(q + 1) * LANES, (t - done) * LANES:(t - done + 1) * LANES]
+                    tops[t] = jnp.maximum(tops[t], highest(tile + biases[q]))
+        done = end
     for n, block in enumerate(order):
         best[block] = jnp.broadcast_to(jnp.max(tops[n], axis=0, keepdims=True), (8, LANES))
 

time: 50.3 us -> 47 us (0.934)
  Pallas kernels: 48.9 us -> 45.6 us
    pallas_call x1, Pallas kernels: 48.9 us -> 45.6 us  [per_device(): pl.pallas_call(functools.partial(kernel, C, F, slot, stack_rows, rows * F...]
where the time goes in v2:
time: 47 us; the launch traced here: 46.9 us
  Pallas kernels  45.6 us (97%)
  local copies, waits for them, and re-layouts  1.26 us (3%)
    pallas_call x1, Pallas kernels, per_device(): pl.pallas_call(functools.partial(kernel, C, F, slot, stack_rows, rows * F...  45.6 us
    unnamed x1, local copies, waits for them, and re-layouts  1.26 us

profile of v2, /device:TPU:0, one launch (start us, length us, event | category | flops | bytes accessed | tf_op | source)
XLA Modules:
  0.0 46.9 jit_solution(11368391722888154710)
XLA Ops:
  0.0 45.6 %shard_map.28 = f32[1,512]{1,0:T(1,128)} custom-call(bf16[512,512]{1,0:T(8,128)(2,1)} %emb_hbm.1, s32[1,512]{1,0:T(1,128)} %bitcast.3), custom_call_target="tpu_custom_call" | custom-call | tf_op jit(solution)/shard_map/pallas_call | solution.py:346
  45.6 1.3 %copy.4 = f32[512]{0:T(512)} copy(f32[512]{0:T(512)} %bitcast.2) | data formatting | bytes 4096

commit v3 on v2

--- a/solution.py
+++ b/solution.py
@@ -69,11 +69,14 @@
     def z_other(k, flip):
         return 2 * z_peer(k) + (1 - core if flip else core)
 
-    steps = sorted(range(1, Z), key=lambda k: min(k, Z - k))
-    far = [z_other(k, flip) for k in steps for flip in (False, True)]
-    early, middle = len(far) // 3, len(far) // 3 + len(far) // 6
-    lots = [far[:early] + [z_other(0, True)], far[early:middle], far[middle + 1:] + [far[middle]]]
-    peers = lots[0] + lots[1] + lots[2]
+    steps = sorted(range(1, Z), key=lambda k: -min(k, Z - k))
+    far = [z_other(steps[0], False)]
+    far += [z_other(k, flip) for k in steps[1:] for flip in (False, True)]
+    far += [z_other(steps[0], True)]
+    cuts = [0, len(far) // 6, len(far) // 3, 2 * len(far) // 3, len(far)]
+    lots = [far[cuts[n]:cuts[n + 1]] for n in range(4)]
+    lots[0].append(z_other(0, True))
+    peers = sum(lots, [])
 
     barrier = pltpu.get_barrier_semaphore()
     for k in range(1, F):
@@ -156,7 +159,7 @@
         row_copy(peer, f).start()
     for peer in peers:
         count_copy(peer, f).start()
-    compact(lots[1] + lots[2] + [f])
+    compact(lots[1] + lots[2] + lots[3] + [f])
     slot_rows(received, f)[...] = slot_rows(outgoing, f)[...]
     counts_in[f] = counts_out[f]
     value = rows_at(half, c * part_rows, part_rows)[...]
@@ -199,15 +202,17 @@
 
     for k in range(1, Z):
         z_gather(z_peer(k), z).start()
+    for k in range(1, Z):
+        z_gather(z_peer(k), z_peer(k)).wait_recv()
+    for k in range(1, C):
+        coarse_gather(coarse_peer(k), c).start()
     for peer in lots[2]:
         row_copy(peer, f).start()
-    for k in range(1, Z):
-        z_gather(z_peer(k), z_peer(k)).wait_recv()
-    for k in range(1, C):
-        coarse_gather(coarse_peer(k), c).start()
     for k in range(1, C):
         coarse_gather(coarse_peer(k), coarse_peer(k)).wait_recv()
     core_gather(core).start()
+    for peer in lots[3]:
+        row_copy(peer, f).start()
 
     for k in range(1, F):
         count_copy(fine_peer(k), fine_peer(k)).wait_recv()
@@ -240,7 +245,7 @@
 
     group = LANES // slot
     if group == 1:
-        batches = [[f] + lots[0] + lots[1], lots[2]]
+        batches = [[f] + lots[0] + lots[1] + lots[2], lots[3]]
     else:
         batches = [[lax.rem(lax.div(f, group) + n, F // group) for n in range(F // group)]]
         for peer in peers:

time: 47 us -> 45.4 us (0.966)
  Pallas kernels: 45.6 us -> 44 us
    pallas_call x1, Pallas kernels: 45.6 us -> 44 us  [per_device(): pl.pallas_call(functools.partial(kernel, C, F, slot, stack_rows, rows * F...]
where the time goes in v3:
time: 45.4 us; the launch traced here: 45.3 us
  Pallas kernels  44 us (97%)
  local copies, waits for them, and re-layouts  1.26 us (3%)
    pallas_call x1, Pallas kernels, per_device(): pl.pallas_call(functools.partial(kernel, C, F, slot, stack_rows, rows * F...  44 us
    unnamed x1, local copies, waits for them, and re-layouts  1.26 us

profile of v3, /device:TPU:0, one launch (start us, length us, event | category | flops | bytes accessed | tf_op | source)
XLA Modules:
  0.0 45.3 jit_solution(12426260638192857168)
XLA Ops:
  0.0 44.0 %shard_map.28 = f32[1,512]{1,0:T(1,128)} custom-call(bf16[512,512]{1,0:T(8,128)(2,1)} %emb_hbm.1, s32[1,512]{1,0:T(1,128)} %bitcast.3), custom_call_target="tpu_custom_call" | custom-call | tf_op jit(solution)/shard_map/pallas_call | solution.py:351
  44.0 1.3 %copy.4 = f32[512]{0:T(512)} copy(f32[512]{0:T(512)} %bitcast.2) | data formatting | bytes 4096

commit v4 on v3

--- a/solution.py
+++ b/solution.py
@@ -73,7 +73,7 @@
     far = [z_other(steps[0], False)]
     far += [z_other(k, flip) for k in steps[1:] for flip in (False, True)]
     far += [z_other(steps[0], True)]
-    cuts = [0, len(far) // 6, len(far) // 3, 2 * len(far) // 3, len(far)]
+    cuts = [0, len(far) // 6, len(far) // 2, 5 * len(far) // 6, len(far)]
     lots = [far[cuts[n]:cuts[n + 1]] for n in range(4)]
     lots[0].append(z_other(0, True))
     peers = sum(lots, [])
@@ -142,8 +142,6 @@
         for n, to in enumerate(devices):
             slot_rows(outgoing, to)[...] = picked[n * slot:(n + 1) * slot, :]
 
-    compact(lots[0])
-
     core_copy.wait_recv()
     half[...] = rows_at(acc, core * half_rows, half_rows)[...] + half_in[...]
 
@@ -155,6 +153,7 @@
 
     for k in range(1, C):
         coarse_copy(coarse_peer(k), c).start()
+    compact(lots[0])
     for peer in lots[0]:
         row_copy(peer, f).start()
     for peer in peers:

time: 45.4 us -> 47.5 us (1.046)
  Pallas kernels: 44 us -> 46 us
    pallas_call x1, Pallas kernels: 44 us -> 46 us  [per_device(): pl.pallas_call(functools.partial(kernel, C, F, slot, stack_rows, rows * F...]
where the time goes in v4:
time: 47.5 us; the launch traced here: 47.3 us
  Pallas kernels  46 us (97%)
  local copies, waits for them, and re-layouts  1.26 us (3%)
    pallas_call x1, Pallas kernels, per_device(): pl.pallas_call(functools.partial(kernel, C, F, slot, stack_rows, rows * F...  46 us
    unnamed x1, local copies, waits for them, and re-layouts  1.26 us

profile of v4, /device:TPU:0, one launch (start us, length us, event | category | flops | bytes accessed | tf_op | source)
XLA Modules:
  0.0 47.3 jit_solution(1139317920728946739)
XLA Ops:
  0.0 46.0 %shard_map.28 = f32[1,512]{1,0:T(1,128)} custom-call(bf16[512,512]{1,0:T(8,128)(2,1)} %emb_hbm.1, s32[1,512]{1,0:T(1,128)} %bitcast.3), custom_call_target="tpu_custom_call" | custom-call | tf_op jit(solution)/shard_map/pallas_call | solution.py:350
  46.0 1.3 %copy.4 = f32[512]{0:T(512)} copy(f32[512]{0:T(512)} %bitcast.2) | data formatting | bytes 4096

commit v5 on v3

--- a/solution.py
+++ b/solution.py
@@ -73,8 +73,8 @@
     far = [z_other(steps[0], False)]
     far += [z_other(k, flip) for k in steps[1:] for flip in (False, True)]
     far += [z_other(steps[0], True)]
-    cuts = [0, len(far) // 6, len(far) // 3, 2 * len(far) // 3, len(far)]
-    lots = [far[cuts[n]:cuts[n + 1]] for n in range(4)]
+    cuts = [0, len(far) // 6, 2 * len(far) // 3, len(far)]
+    lots = [far[cuts[n]:cuts[n + 1]] for n in range(3)]
     lots[0].append(z_other(0, True))
     peers = sum(lots, [])
 
@@ -159,7 +159,7 @@
         row_copy(peer, f).start()
     for peer in peers:
         count_copy(peer, f).start()
-    compact(lots[1] + lots[2] + lots[3] + [f])
+    compact(lots[1] + lots[2] + [f])
     slot_rows(received, f)[...] = slot_rows(outgoing, f)[...]
     counts_in[f] = counts_out[f]
     value = rows_at(half, c * part_rows, part_rows)[...]
@@ -176,8 +176,6 @@
 
     for k in range(1, Z):
         z_copy(z_peer(k), z).start()
-    for peer in lots[1]:
-        row_copy(peer, f).start()
     value = rows_at(part, z * piece_rows, piece_rows)[...]
     for k in range(1, Z):
         z_copy(z_peer(k), z_peer(k)).wait_recv()
@@ -206,12 +204,12 @@
         z_gather(z_peer(k), z_peer(k)).wait_recv()
     for k in range(1, C):
         coarse_gather(coarse_peer(k), c).start()
-    for peer in lots[2]:
+    for peer in lots[1]:
         row_copy(peer, f).start()
     for k in range(1, C):
         coarse_gather(coarse_peer(k), coarse_peer(k)).wait_recv()
     core_gather(core).start()
-    for peer in lots[3]:
+    for peer in lots[2]:
         row_copy(peer, f).start()
 
     for k in range(1, F):
@@ -245,7 +243,7 @@
 
     group = LANES // slot
     if group == 1:
-        batches = [[f] + lots[0] + lots[1] + lots[2], lots[3]]
+        batches = [[f] + lots[0] + lots[1], lots[2]]
     else:
         batches = [[lax.rem(lax.div(f, group) + n, F // group) for n in range(F // group)]]
         for peer in peers:

time: 45.4 us -> 44.6 us (0.982)
  Pallas kernels: 44 us -> 43.2 us
    pallas_call x1, Pallas kernels: 44 us -> 43.2 us  [per_device(): pl.pallas_call(functools.partial(kernel, C, F, slot, stack_rows, rows * F...]
where the time goes in v5:
time: 44.6 us; the launch traced here: 44.4 us
  Pallas kernels  43.2 us (97%)
  local copies, waits for them, and re-layouts  1.26 us (3%)
    pallas_call x1, Pallas kernels, per_device(): pl.pallas_call(functools.partial(kernel, C, F, slot, stack_rows, rows * F...  43.2 us
    unnamed x1, local copies, waits for them, and re-layouts  1.26 us

profile of v5, /device:TPU:0, one launch (start us, length us, event | category | flops | bytes accessed | tf_op | source)
XLA Modules:
  0.0 44.4 jit_solution(16379179412767943452)
XLA Ops:
  0.0 43.2 %shard_map.28 = f32[1,512]{1,0:T(1,128)} custom-call(bf16[512,512]{1,0:T(8,128)(2,1)} %emb_hbm.1, s32[1,512]{1,0:T(1,128)} %bitcast.3), custom_call_target="tpu_custom_call" | custom-call | tf_op jit(solution)/shard_map/pallas_call | solution.py:349
  43.2 1.3 %copy.4 = f32[512]{0:T(512)} copy(f32[512]{0:T(512)} %bitcast.2) | data formatting | bytes 4096

commit v6 on v5

--- a/solution.py
+++ b/solution.py
@@ -73,7 +73,7 @@
     far = [z_other(steps[0], False)]
     far += [z_other(k, flip) for k in steps[1:] for flip in (False, True)]
     far += [z_other(steps[0], True)]
-    cuts = [0, len(far) // 6, 2 * len(far) // 3, len(far)]
+    cuts = [0, len(far) // 6, 5 * len(far) // 6, len(far)]
     lots = [far[cuts[n]:cuts[n + 1]] for n in range(3)]
     lots[0].append(z_other(0, True))
     peers = sum(lots, [])

time: 44.6 us -> 44.3 us (level)
  no operation moved by 1% of the time
where the time goes in v6:
time: 44.3 us; the launch traced here: 44.1 us
  Pallas kernels  42.9 us (97%)
  local copies, waits for them, and re-layouts  1.26 us (3%)
    pallas_call x1, Pallas kernels, per_device(): pl.pallas_call(functools.partial(kernel, C, F, slot, stack_rows, rows * F...  42.9 us
    unnamed x1, local copies, waits for them, and re-layouts  1.26 us

profile of v6, /device:TPU:0, one launch (start us, length us, event | category | flops | bytes accessed | tf_op | source)
XLA Modules:
  0.0 44.1 jit_solution(16688569279907783061)
XLA Ops:
  0.0 42.9 %shard_map.28 = f32[1,512]{1,0:T(1,128)} custom-call(bf16[512,512]{1,0:T(8,128)(2,1)} %emb_hbm.1, s32[1,512]{1,0:T(1,128)} %bitcast.3), custom_call_target="tpu_custom_call" | custom-call | tf_op jit(solution)/shard_map/pallas_call | solution.py:349
  42.9 1.3 %copy.4 = f32[512]{0:T(512)} copy(f32[512]{0:T(512)} %bitcast.2) | data formatting | bytes 4096
